TPU v7x, 32 devices: a whole 2x2x4 slice. The times are simulated.
32 devices in a mesh: parts: 2 (over x), shift: 16 (over z, y, core).
Axes of the slice: x: 2, y: 2, z: 4, core: 2. Of those that a mesh axis runs over, the one named last changes fastest.
Arguments:
- embeddings: bfloat16 [16384, 768], P(('parts', 'shift')), parts along dimension 0, as said below
- block_cluster: int32 [128], P(('parts', 'shift')), parts along dimension 0, may hold values from 0 to 7, never falling along the last dimension, each value on 1 to 16 neighbouring positions
Outputs:
- best_match: float32 [16384], P(('parts', 'shift')), parts along dimension 0
There are 2 independent parts, one for each index of `parts`. A program takes and returns all parts, laid end to end along the dimension named above; each array names one. Nothing has to cross between parts.
Inputs may be any that keep to these rules, and one draw needn't show every extreme that they name: block_cluster never falls along the blocks; each cluster holds 1 to 16 consecutive blocks and one holds exactly 16. `embeddings`: every row is nonzero; rows may differ in scale, which the first step removes.
All inputs are finite; a program needn't handle non-finite values.
Results may differ from a plain program's by a relative error of at most 0.00059.
Values may be sent and summed in bfloat16 or wider, within the bound.
No kernel may reach another device: no remote copies, remote signals or barrier semaphores. Data moves between devices by JAX's collectives and lax.ppermute only.
A program may use at most 64 MiB of HBM per device.

v0:
```python
import math

import jax
import jax.numpy as jnp
from jax import lax
from jax.sharding import PartitionSpec as P


def passed_along(array, axis, by):
    length = lax.axis_size(axis)
    return lax.ppermute(array, axis, [(i, (i + by) % length) for i in range(length)])


def normalize(embeddings):
    values = embeddings.astype(jnp.float32)
    scale = lax.rsqrt(jnp.mean(values * values, axis=1, keepdims=True) + 1e-06) / math.sqrt(
        embeddings.shape[1]
    )
    return (values * scale).astype(jnp.bfloat16)


def local(embeddings, block_cluster):
    rows = embeddings.shape[0]
    blocks = block_cluster.shape[0]
    width = rows // blocks
    count = lax.axis_size("shift")
    mine = lax.axis_index("shift")
    unit = normalize(embeddings)
    table = lax.all_gather(block_cluster, "shift", axis=0, tiled=True)
    own_cluster = jnp.repeat(block_cluster, width)
    offsets = jnp.arange(rows, dtype=jnp.int32)
    own_rows = mine * rows + offsets

    def visit(best, visitor, source, valid):
        safe = jnp.clip(source, 0, count - 1)
        ids = lax.dynamic_slice_in_dim(table, safe * blocks, blocks)
        far_cluster = jnp.repeat(ids, width)
        far_rows = safe * rows + offsets
        sims = lax.dot_general(
            unit, visitor, (((1,), (1,)), ((), ())), preferred_element_type=jnp.float32
        )
        mask = (
            (own_cluster[:, None] == far_cluster[None, :])
            & (own_rows[:, None] != far_rows[None, :])
            & valid
        )
        return jnp.maximum(best, jnp.max(jnp.where(mask, sims, jnp.float32(-2.0)), axis=1))

    best = visit(jnp.full((rows,), -1.0, jnp.float32), unit, mine, jnp.asarray(True))

    def step(turn, carry):
        current, visitor = carry
        visitor = passed_along(visitor, "shift", 1)
        source = (mine - turn) % count
        return (visit(current, visitor, source, jnp.asarray(True)), visitor)

    best, unused = lax.fori_loop(1, count, step, (best, unit))
    return best


def solution(mesh):
    return jax.shard_map(
        local,
        mesh=mesh,
        in_specs=(P(("parts", "shift"), None), P(("parts", "shift"))),
        out_specs=P(("parts", "shift")),
        check_vma=False,
    )
```

profile of v0, /device:TPU:0, one launch (start us, length us, event | category | flops | bytes accessed | tf_op | source)
XLA Modules:
  0.0 242.4 jit_solution(2436069734255851284)
XLA Ops:
  0.0 1.4 fusion.7
  3.7 13.7 %all-reduce = s32[64]{0:T(128)S(1)} all-reduce(s32[64]{0:T(128)S(1)} %dynamic-update-slice), channel_id=1, replica_groups=mesh['parts'=2,'shift'=16] {'shift'}, use_global_device_ids=true, to_apply=%add | all-reduce | flops 64 | bytes 512
  17.6 0.7 fusion.9
  18.3 223.5 %while.18 = (s32[]{:T(128)}, f32[512]{0:T(512)S(1)}, bf16[512,768]{1,0:T(8,128)(2,1)S(1)}, s32[]{:T(128)}, s32[64]{0:T(128)S(1)}, /*index=5*/bf16[512,768]{1,0:T...) while((s32[]{:T(128)}, f32[512]{0:T(512)S(1)}, ...), condition=%wide.region_4.5_spmd.clone, body=%wide.region_2.4_spmd.clone.sunk | while | flops 403964960 | bytes 6316492 | solution.py:57
  18.5 13.9 %collective-permute-done = bf16[512,768]{1,0:T(8,128)(2,1)S(1)} collective-permute-done((bf16[512,768]{1,0:T(8,128)(2,1)S(1)}, bf16[512,768]{1,0:T(8,128)(2,1)S(1)}, u32[]{:S(2)}, u32[]{:S(2)}) %collective-permute-start) | collective-permute-done | bytes 786464 | tf_op jit(solution)/shard_map/while/body/eval_jaxpr/ppermute | solution.py:11
  33.4 13.9 %collective-permute-done = bf16[512,768]{1,0:T(8,128)(2,1)S(1)} collective-permute-done((bf16[512,768]{1,0:T(8,128)(2,1)S(1)}, bf16[512,768]{1,0:T(8,128)(2,1)S(1)}, u32[]{:S(2)}, u32[]{:S(2)}) %collective-permute-start) | collective-permute-done | bytes 786464 | tf_op jit(solution)/shard_map/while/body/eval_jaxpr/ppermute | solution.py:11
  47.4 0.6 fusion.19
  48.3 13.9 %collective-permute-done = bf16[512,768]{1,0:T(8,128)(2,1)S(1)} collective-permute-done((bf16[512,768]{1,0:T(8,128)(2,1)S(1)}, bf16[512,768]{1,0:T(8,128)(2,1)S(1)}, u32[]{:S(2)}, u32[]{:S(2)}) %collective-permute-start) | collective-permute-done | bytes 786464 | tf_op jit(solution)/shard_map/while/body/eval_jaxpr/ppermute | solution.py:11
  63.2 13.9 %collective-permute-done = bf16[512,768]{1,0:T(8,128)(2,1)S(1)} collective-permute-done((bf16[512,768]{1,0:T(8,128)(2,1)S(1)}, bf16[512,768]{1,0:T(8,128)(2,1)S(1)}, u32[]{:S(2)}, u32[]{:S(2)}) %collective-permute-start) | collective-permute-done | bytes 786464 | tf_op jit(solution)/shard_map/while/body/eval_jaxpr/ppermute | solution.py:11
  78.1 13.9 %collective-permute-done = bf16[512,768]{1,0:T(8,128)(2,1)S(1)} collective-permute-done((bf16[512,768]{1,0:T(8,128)(2,1)S(1)}, bf16[512,768]{1,0:T(8,128)(2,1)S(1)}, u32[]{:S(2)}, u32[]{:S(2)}) %collective-permute-start) | collective-permute-done | bytes 786464 | tf_op jit(solution)/shard_map/while/body/eval_jaxpr/ppermute | solution.py:11
  92.1 0.7 fusion.19
  93.0 13.9 %collective-permute-done = bf16[512,768]{1,0:T(8,128)(2,1)S(1)} collective-permute-done((bf16[512,768]{1,0:T(8,128)(2,1)S(1)}, bf16[512,768]{1,0:T(8,128)(2,1)S(1)}, u32[]{:S(2)}, u32[]{:S(2)}) %collective-permute-start) | collective-permute-done | bytes 786464 | tf_op jit(solution)/shard_map/while/body/eval_jaxpr/ppermute | solution.py:11
  107.9 13.9 %collective-permute-done = bf16[512,768]{1,0:T(8,128)(2,1)S(1)} collective-permute-done((bf16[512,768]{1,0:T(8,128)(2,1)S(1)}, bf16[512,768]{1,0:T(8,128)(2,1)S(1)}, u32[]{:S(2)}, u32[]{:S(2)}) %collective-permute-start) | collective-permute-done | bytes 786464 | tf_op jit(solution)/shard_map/while/body/eval_jaxpr/ppermute | solution.py:11
  121.9 0.6 fusion.19
  122.8 13.9 %collective-permute-done = bf16[512,768]{1,0:T(8,128)(2,1)S(1)} collective-permute-done((bf16[512,768]{1,0:T(8,128)(2,1)S(1)}, bf16[512,768]{1,0:T(8,128)(2,1)S(1)}, u32[]{:S(2)}, u32[]{:S(2)}) %collective-permute-start) | collective-permute-done | bytes 786464 | tf_op jit(solution)/shard_map/while/body/eval_jaxpr/ppermute | solution.py:11
  137.7 13.9 %collective-permute-done = bf16[512,768]{1,0:T(8,128)(2,1)S(1)} collective-permute-done((bf16[512,768]{1,0:T(8,128)(2,1)S(1)}, bf16[512,768]{1,0:T(8,128)(2,1)S(1)}, u32[]{:S(2)}, u32[]{:S(2)}) %collective-permute-start) | collective-permute-done | bytes 786464 | tf_op jit(solution)/shard_map/while/body/eval_jaxpr/ppermute | solution.py:11
  152.6 13.9 %collective-permute-done = bf16[512,768]{1,0:T(8,128)(2,1)S(1)} collective-permute-done((bf16[512,768]{1,0:T(8,128)(2,1)S(1)}, bf16[512,768]{1,0:T(8,128)(2,1)S(1)}, u32[]{:S(2)}, u32[]{:S(2)}) %collective-permute-start) | collective-permute-done | bytes 786464 | tf_op jit(solution)/shard_map/while/body/eval_jaxpr/ppermute | solution.py:11
  166.6 0.7 fusion.19
  167.6 13.9 %collective-permute-done = bf16[512,768]{1,0:T(8,128)(2,1)S(1)} collective-permute-done((bf16[512,768]{1,0:T(8,128)(2,1)S(1)}, bf16[512,768]{1,0:T(8,128)(2,1)S(1)}, u32[]{:S(2)}, u32[]{:S(2)}) %collective-permute-start) | collective-permute-done | bytes 786464 | tf_op jit(solution)/shard_map/while/body/eval_jaxpr/ppermute | solution.py:11
  182.4 13.9 %collective-permute-done = bf16[512,768]{1,0:T(8,128)(2,1)S(1)} collective-permute-done((bf16[512,768]{1,0:T(8,128)(2,1)S(1)}, bf16[512,768]{1,0:T(8,128)(2,1)S(1)}, u32[]{:S(2)}, u32[]{:S(2)}) %collective-permute-start) | collective-permute-done | bytes 786464 | tf_op jit(solution)/shard_map/while/body/eval_jaxpr/ppermute | solution.py:11
  197.3 13.9 %collective-permute-done = bf16[512,768]{1,0:T(8,128)(2,1)S(1)} collective-permute-done((bf16[512,768]{1,0:T(8,128)(2,1)S(1)}, bf16[512,768]{1,0:T(8,128)(2,1)S(1)}, u32[]{:S(2)}, u32[]{:S(2)}) %collective-permute-start) | collective-permute-done | bytes 786464 | tf_op jit(solution)/shard_map/while/body/eval_jaxpr/ppermute | solution.py:11
  212.3 13.9 %collective-permute-done = bf16[512,768]{1,0:T(8,128)(2,1)S(1)} collective-permute-done((bf16[512,768]{1,0:T(8,128)(2,1)S(1)}, bf16[512,768]{1,0:T(8,128)(2,1)S(1)}, u32[]{:S(2)}, u32[]{:S(2)}) %collective-permute-start) | collective-permute-done | bytes 786464 | tf_op jit(solution)/shard_map/while/body/eval_jaxpr/ppermute | solution.py:11
  227.1 13.9 %collective-permute-done = bf16[512,768]{1,0:T(8,128)(2,1)S(1)} collective-permute-done((bf16[512,768]{1,0:T(8,128)(2,1)S(1)}, bf16[512,768]{1,0:T(8,128)(2,1)S(1)}, u32[]{:S(2)}, u32[]{:S(2)}) %collective-permute-start) | collective-permute-done | bytes 786464 | tf_op jit(solution)/shard_map/while/body/eval_jaxpr/ppermute | solution.py:11
  241.1 0.7 fusion.19
  (119 shorter events, 12.9 us)
Async XLA Ops:
  0.0 1.5 copy-start
  1.5 0.7 copy-start.2
  1.5 0.7 copy-start.3
  18.3 14.2 %collective-permute-start = (bf16[512,768]{1,0:T(8,128)(2,1)S(1)}, bf16[512,768]{1,0:T(8,128)(2,1)S(1)}, u32[]{:S(2)}, u32[]{:S(2)}) collective-permute-start(bf16[512,768]{1,0:T(8,128)(2,1)S(1)} %get-tuple-element.345), channel_id=1, source_target_pairs={{0,1},{1,2},{2,3},{3,4},{4,5},{5,6},{6,7},{7,8},{8,9},{9,10},{10,1... | collective-permute-start | bytes 2359304 | tf_op jit(solution)/shard_map/while/body/eval_jaxpr/ppermute | solution.py:11
  33.2 14.2 %collective-permute-start = (bf16[512,768]{1,0:T(8,128)(2,1)S(1)}, bf16[512,768]{1,0:T(8,128)(2,1)S(1)}, u32[]{:S(2)}, u32[]{:S(2)}) collective-permute-start(bf16[512,768]{1,0:T(8,128)(2,1)S(1)} %get-tuple-element.345), channel_id=1, source_target_pairs={{0,1},{1,2},{2,3},{3,4},{4,5},{5,6},{6,7},{7,8},{8,9},{9,10},{10,1... | collective-permute-start | bytes 2359304 | tf_op jit(solution)/shard_map/while/body/eval_jaxpr/ppermute | solution.py:11
  48.1 14.2 %collective-permute-start = (bf16[512,768]{1,0:T(8,128)(2,1)S(1)}, bf16[512,768]{1,0:T(8,128)(2,1)S(1)}, u32[]{:S(2)}, u32[]{:S(2)}) collective-permute-start(bf16[512,768]{1,0:T(8,128)(2,1)S(1)} %get-tuple-element.345), channel_id=1, source_target_pairs={{0,1},{1,2},{2,3},{3,4},{4,5},{5,6},{6,7},{7,8},{8,9},{9,10},{10,1... | collective-permute-start | bytes 2359304 | tf_op jit(solution)/shard_map/while/body/eval_jaxpr/ppermute | solution.py:11
  63.0 14.2 %collective-permute-start = (bf16[512,768]{1,0:T(8,128)(2,1)S(1)}, bf16[512,768]{1,0:T(8,128)(2,1)S(1)}, u32[]{:S(2)}, u32[]{:S(2)}) collective-permute-start(bf16[512,768]{1,0:T(8,128)(2,1)S(1)} %get-tuple-element.345), channel_id=1, source_target_pairs={{0,1},{1,2},{2,3},{3,4},{4,5},{5,6},{6,7},{7,8},{8,9},{9,10},{10,1... | collective-permute-start | bytes 2359304 | tf_op jit(solution)/shard_map/while/body/eval_jaxpr/ppermute | solution.py:11
  77.9 14.2 %collective-permute-start = (bf16[512,768]{1,0:T(8,128)(2,1)S(1)}, bf16[512,768]{1,0:T(8,128)(2,1)S(1)}, u32[]{:S(2)}, u32[]{:S(2)}) collective-permute-start(bf16[512,768]{1,0:T(8,128)(2,1)S(1)} %get-tuple-element.345), channel_id=1, source_target_pairs={{0,1},{1,2},{2,3},{3,4},{4,5},{5,6},{6,7},{7,8},{8,9},{9,10},{10,1... | collective-permute-start | bytes 2359304 | tf_op jit(solution)/shard_map/while/body/eval_jaxpr/ppermute | solution.py:11
  92.8 14.2 %collective-permute-start = (bf16[512,768]{1,0:T(8,128)(2,1)S(1)}, bf16[512,768]{1,0:T(8,128)(2,1)S(1)}, u32[]{:S(2)}, u32[]{:S(2)}) collective-permute-start(bf16[512,768]{1,0:T(8,128)(2,1)S(1)} %get-tuple-element.345), channel_id=1, source_target_pairs={{0,1},{1,2},{2,3},{3,4},{4,5},{5,6},{6,7},{7,8},{8,9},{9,10},{10,1... | collective-permute-start | bytes 2359304 | tf_op jit(solution)/shard_map/while/body/eval_jaxpr/ppermute | solution.py:11
  107.7 14.2 %collective-permute-start = (bf16[512,768]{1,0:T(8,128)(2,1)S(1)}, bf16[512,768]{1,0:T(8,128)(2,1)S(1)}, u32[]{:S(2)}, u32[]{:S(2)}) collective-permute-start(bf16[512,768]{1,0:T(8,128)(2,1)S(1)} %get-tuple-element.345), channel_id=1, source_target_pairs={{0,1},{1,2},{2,3},{3,4},{4,5},{5,6},{6,7},{7,8},{8,9},{9,10},{10,1... | collective-permute-start | bytes 2359304 | tf_op jit(solution)/shard_map/while/body/eval_jaxpr/ppermute | solution.py:11
  122.6 14.2 %collective-permute-start = (bf16[512,768]{1,0:T(8,128)(2,1)S(1)}, bf16[512,768]{1,0:T(8,128)(2,1)S(1)}, u32[]{:S(2)}, u32[]{:S(2)}) collective-permute-start(bf16[512,768]{1,0:T(8,128)(2,1)S(1)} %get-tuple-element.345), channel_id=1, source_target_pairs={{0,1},{1,2},{2,3},{3,4},{4,5},{5,6},{6,7},{7,8},{8,9},{9,10},{10,1... | collective-permute-start | bytes 2359304 | tf_op jit(solution)/shard_map/while/body/eval_jaxpr/ppermute | solution.py:11
  137.5 14.2 %collective-permute-start = (bf16[512,768]{1,0:T(8,128)(2,1)S(1)}, bf16[512,768]{1,0:T(8,128)(2,1)S(1)}, u32[]{:S(2)}, u32[]{:S(2)}) collective-permute-start(bf16[512,768]{1,0:T(8,128)(2,1)S(1)} %get-tuple-element.345), channel_id=1, source_target_pairs={{0,1},{1,2},{2,3},{3,4},{4,5},{5,6},{6,7},{7,8},{8,9},{9,10},{10,1... | collective-permute-start | bytes 2359304 | tf_op jit(solution)/shard_map/while/body/eval_jaxpr/ppermute | solution.py:11
  152.4 14.2 %collective-permute-start = (bf16[512,768]{1,0:T(8,128)(2,1)S(1)}, bf16[512,768]{1,0:T(8,128)(2,1)S(1)}, u32[]{:S(2)}, u32[]{:S(2)}) collective-permute-start(bf16[512,768]{1,0:T(8,128)(2,1)S(1)} %get-tuple-element.345), channel_id=1, source_target_pairs={{0,1},{1,2},{2,3},{3,4},{4,5},{5,6},{6,7},{7,8},{8,9},{9,10},{10,1... | collective-permute-start | bytes 2359304 | tf_op jit(solution)/shard_map/while/body/eval_jaxpr/ppermute | solution.py:11
  167.3 14.2 %collective-permute-start = (bf16[512,768]{1,0:T(8,128)(2,1)S(1)}, bf16[512,768]{1,0:T(8,128)(2,1)S(1)}, u32[]{:S(2)}, u32[]{:S(2)}) collective-permute-start(bf16[512,768]{1,0:T(8,128)(2,1)S(1)} %get-tuple-element.345), channel_id=1, source_target_pairs={{0,1},{1,2},{2,3},{3,4},{4,5},{5,6},{6,7},{7,8},{8,9},{9,10},{10,1... | collective-permute-start | bytes 2359304 | tf_op jit(solution)/shard_map/while/body/eval_jaxpr/ppermute | solution.py:11
  182.2 14.2 %collective-permute-start = (bf16[512,768]{1,0:T(8,128)(2,1)S(1)}, bf16[512,768]{1,0:T(8,128)(2,1)S(1)}, u32[]{:S(2)}, u32[]{:S(2)}) collective-permute-start(bf16[512,768]{1,0:T(8,128)(2,1)S(1)} %get-tuple-element.345), channel_id=1, source_target_pairs={{0,1},{1,2},{2,3},{3,4},{4,5},{5,6},{6,7},{7,8},{8,9},{9,10},{10,1... | collective-permute-start | bytes 2359304 | tf_op jit(solution)/shard_map/while/body/eval_jaxpr/ppermute | solution.py:11
  197.1 14.2 %collective-permute-start = (bf16[512,768]{1,0:T(8,128)(2,1)S(1)}, bf16[512,768]{1,0:T(8,128)(2,1)S(1)}, u32[]{:S(2)}, u32[]{:S(2)}) collective-permute-start(bf16[512,768]{1,0:T(8,128)(2,1)S(1)} %get-tuple-element.345), channel_id=1, source_target_pairs={{0,1},{1,2},{2,3},{3,4},{4,5},{5,6},{6,7},{7,8},{8,9},{9,10},{10,1... | collective-permute-start | bytes 2359304 | tf_op jit(solution)/shard_map/while/body/eval_jaxpr/ppermute | solution.py:11
  212.0 14.2 %collective-permute-start = (bf16[512,768]{1,0:T(8,128)(2,1)S(1)}, bf16[512,768]{1,0:T(8,128)(2,1)S(1)}, u32[]{:S(2)}, u32[]{:S(2)}) collective-permute-start(bf16[512,768]{1,0:T(8,128)(2,1)S(1)} %get-tuple-element.345), channel_id=1, source_target_pairs={{0,1},{1,2},{2,3},{3,4},{4,5},{5,6},{6,7},{7,8},{8,9},{9,10},{10,1... | collective-permute-start | bytes 2359304 | tf_op jit(solution)/shard_map/while/body/eval_jaxpr/ppermute | solution.py:11
  226.9 14.2 %collective-permute-start = (bf16[512,768]{1,0:T(8,128)(2,1)S(1)}, bf16[512,768]{1,0:T(8,128)(2,1)S(1)}, u32[]{:S(2)}, u32[]{:S(2)}) collective-permute-start(bf16[512,768]{1,0:T(8,128)(2,1)S(1)} %get-tuple-element.345), channel_id=1, source_target_pairs={{0,1},{1,2},{2,3},{3,4},{4,5},{5,6},{6,7},{7,8},{8,9},{9,10},{10,1... | collective-permute-start | bytes 2359304 | tf_op jit(solution)/shard_map/while/body/eval_jaxpr/ppermute | solution.py:11
  241.8 0.6 copy-start.1
where the time goes:
time: 243 us; the launch traced here: 242 us
  waiting for transfers between devices  209 us (86%)
  blocking collectives  13.7 us (6%)
  matrix products  10.4 us (4%)
  local copies, waits for them, and re-layouts  5.1 us (2%)
    ppermute x15, waiting for transfers between devices, passed_along(): lax.ppermute(array, axis, [(i, (i + by) % length) for i in range(length)])  209 us
    unnamed x1, blocking collectives  13.7 us
    dot_general x16, matrix products, visit(): lax.dot_general(unit, visitor, (((1,), (1,)), ((), ())), preferred_elemen...  10.4 us
  transfers between devices with their start and end apart: 15, of which 15 were waited for; matrix products, arithmetic and copies ran while one was open for 1% of the time, Pallas kernels for 0%

commit v1 on v0

v1 whole, which is shorter than its diff:
```python
import functools
import math

import jax
import jax.numpy as jnp
from jax import lax
from jax.experimental import pallas as pl
from jax.experimental.pallas import tpu as pltpu
from jax.sharding import PartitionSpec as P

LOW = -2.0
QUAD = 4


def swapped(array, mask):
    length = lax.axis_size("shift")
    return lax.ppermute(array, "shift", [(i, i ^ mask) for i in range(length)])


def moved(array, by):
    length = lax.axis_size("shift")
    pairs = [(i, i + by) for i in range(length) if 0 <= i + by < length]
    return lax.ppermute(array, "shift", pairs)


def unit_rows(raw):
    values = raw.astype(jnp.float32)
    scale = lax.rsqrt(jnp.mean(values * values, axis=1, keepdims=True) + 1e-06) / math.sqrt(
        raw.shape[1]
    )
    return (values * scale).astype(jnp.bfloat16)


def product(rows, columns):
    return lax.dot_general(
        rows, columns, (((1,), (1,)), ((), ())), preferred_element_type=jnp.float32
    )


def shares(ids, p, q, blocks):
    hit = ids[p, 0] == ids[q, 0]
    for a in range(blocks):
        for b in range(blocks):
            hit = jnp.logical_or(hit, ids[p, a] == ids[q, b])
    return hit


def column_best(ids, p, q, sims, blocks, width, own=False):
    pieces = []
    for b in range(blocks):
        top = jnp.full((8, width), LOW, jnp.float32)
        for a in range(blocks):
            tile = sims[a * width : (a + 1) * width, b * width : (b + 1) * width]
            if own and a == b:
                same = lax.broadcasted_iota(jnp.int32, (width, width), 0) == (
                    lax.broadcasted_iota(jnp.int32, (width, width), 1)
                )
                tile = jnp.where(same, LOW, tile)
            part = jnp.max(tile.reshape(width // 8, 8, width), axis=0)
            top = jnp.maximum(top, jnp.where(ids[p, a] == ids[q, b], part, LOW))
        pieces.append(jnp.max(top, axis=0, keepdims=True))
    return jnp.concatenate(pieces, axis=1)


def row_best(ids, p, q, sims, blocks, width):
    pieces = []
    for a in range(blocks):
        top = jnp.full((width, width), LOW, jnp.float32)
        for b in range(blocks):
            tile = sims[a * width : (a + 1) * width, b * width : (b + 1) * width]
            top = jnp.maximum(top, jnp.where(ids[p, a] == ids[q, b], tile, LOW))
        pieces.append(jnp.max(top.T, axis=0, keepdims=True))
    return jnp.concatenate(pieces, axis=1)


def near_kernel(blocks, ids, own_ref, mate_ref, own_unit, mate_unit, best):
    rows = own_ref.shape[0]
    width = rows // blocks
    own_unit[...] = unit_rows(own_ref[...])
    mate_unit[...] = unit_rows(mate_ref[...])
    sims = product(own_unit[...], own_unit[...])
    best[...] = column_best(ids, 0, 0, sims, blocks, width, own=True)

    @pl.when(shares(ids, 1, 0, blocks))
    def _():
        sims = product(mate_unit[...], own_unit[...])
        best[...] = jnp.maximum(best[...], column_best(ids, 1, 0, sims, blocks, width))


def partner_kernel(blocks, ids, own_unit, partner_ref, best_in, partner_unit, best):
    rows = own_unit.shape[0]
    width = rows // blocks
    partner_unit[...] = unit_rows(partner_ref[...])
    best[...] = best_in[...]

    @pl.when(shares(ids, 2, 0, blocks))
    def _():
        sims = product(partner_unit[...], own_unit[...])
        best[...] = jnp.maximum(best[...], column_best(ids, 2, 0, sims, blocks, width))


def far_kernel(
    blocks, ids, own_unit, mate_unit, partner_unit, cross_ref, back_ref, best_in,
    best, far, back, cross_unit, back_unit,
):
    rows = own_unit.shape[0]
    width = rows // blocks
    cross_unit[...] = unit_rows(cross_ref[...])
    back_unit[...] = unit_rows(back_ref[...])
    best[...] = best_in[...]
    back[...] = jnp.full_like(back, LOW)
    far[...] = jnp.full_like(far, LOW)

    @pl.when(shares(ids, 3, 0, blocks))
    def _():
        sims = product(cross_unit[...], own_unit[...])
        best[...] = jnp.maximum(best[...], column_best(ids, 3, 0, sims, blocks, width))

    for q, held in enumerate((own_unit, mate_unit, partner_unit, cross_unit)):

        @pl.when(shares(ids, q, 4, blocks))
        def _(q=q, held=held):
            sims = product(held[...], back_unit[...])
            back[...] = jnp.maximum(back[...], column_best(ids, q, 4, sims, blocks, width))
            mine = row_best(ids, q, 4, sims, blocks, width)
            if q == 0:
                best[...] = jnp.maximum(best[...], mine)
            else:
                far[q - 1 : q, :] = mine


def local(embeddings, block_cluster):
    rows, depth = embeddings.shape
    blocks = block_cluster.shape[0]
    count = lax.axis_size("shift")
    mine = lax.axis_index("shift")

    partner_raw = swapped(embeddings, 2)
    back_raw = moved(embeddings, QUAD)
    mate_raw = swapped(embeddings, 1)
    own_ids = block_cluster + 1
    ids = jnp.stack(
        [
            own_ids,
            swapped(own_ids, 1),
            swapped(own_ids, 2),
            swapped(own_ids, 3),
            moved(own_ids, QUAD),
        ]
    )

    smem = pl.BlockSpec(memory_space=pltpu.SMEM)
    vmem = pl.BlockSpec(memory_space=pltpu.VMEM)
    units = jax.ShapeDtypeStruct((rows, depth), jnp.bfloat16)
    line = jax.ShapeDtypeStruct((1, rows), jnp.float32)
    params = pltpu.CompilerParams(vmem_limit_bytes=48 * 1024 * 1024)
    flops = 2 * rows * rows * depth

    own_unit, mate_unit, best = pl.pallas_call(
        functools.partial(near_kernel, blocks),
        out_shape=(units, units, line),
        in_specs=[smem, vmem, vmem],
        out_specs=(vmem, vmem, vmem),
        compiler_params=params,
        cost_estimate=pl.CostEstimate(flops=2 * flops, bytes_accessed=8 * rows * depth, transcendentals=0),
    )(ids, embeddings, mate_raw)

    cross_raw = swapped(partner_raw, 1)
    partner_unit, best = pl.pallas_call(
        functools.partial(partner_kernel, blocks),
        out_shape=(units, line),
        in_specs=[smem, vmem, vmem, vmem],
        out_specs=(vmem, vmem),
        compiler_params=params,
        cost_estimate=pl.CostEstimate(flops=flops, bytes_accessed=6 * rows * depth, transcendentals=0),
    )(ids, own_unit, partner_raw, best)

    best, far, back = pl.pallas_call(
        functools.partial(far_kernel, blocks),
        out_shape=(line, jax.ShapeDtypeStruct((3, rows), jnp.float32), line),
        in_specs=[smem] + [vmem] * 6,
        out_specs=(vmem, vmem, vmem),
        scratch_shapes=[
            pltpu.VMEM((rows, depth), jnp.bfloat16),
            pltpu.VMEM((rows, depth), jnp.bfloat16),
        ],
        compiler_params=params,
        cost_estimate=pl.CostEstimate(flops=5 * flops, bytes_accessed=10 * rows * depth, transcendentals=0),
    )(ids, own_unit, mate_unit, partner_unit, cross_raw, back_raw, best)

    from_next = moved(back, -QUAD)
    from_next = jnp.where(mine + QUAD < count, from_next, LOW)
    from_mate = swapped(jnp.concatenate([far[0:1], far[2:3]]), 1)
    from_partner = swapped(jnp.maximum(far[1:2], from_mate[1:2]), 2)
    best = jnp.maximum(jnp.maximum(best, from_next), jnp.maximum(from_mate[0:1], from_partner))
    return jnp.maximum(best.reshape(rows), -1.0)


def solution(mesh):
    return jax.shard_map(
        local,
        mesh=mesh,
        in_specs=(P(("parts", "shift"), None), P(("parts", "shift"))),
        out_specs=P(("parts", "shift")),
        check_vma=False,
    )
```

time: 243 us -> 43.5 us (0.18)
  waiting for transfers between devices: 209 us -> 19.2 us
  starting transfers between devices: 0.87 us -> 16.2 us
  blocking collectives: 13.7 us -> 0 us
  matrix products: 10.4 us -> 0 us
  Pallas kernels: 0 us -> 5.43 us
  local copies, waits for them, and re-layouts: 5.1 us -> 1.16 us
    ppermute x15 -> x11, waiting for transfers between devices: 209 us -> 19.2 us  [the longest x8 15.2 us: swapped(): return lax.ppermute(array, 'shift', [(i, i ^ mask) for i in range(length)])]
    ppermute x15 -> x11, starting transfers between devices: 0.87 us -> 16.2 us  [the longest x3 8.51 us: moved(): return lax.ppermute(array, 'shift', pairs)]
    unnamed x1 -> x0, blocking collectives: 13.7 us -> none
    dot_general x16 -> x0, matrix products: 10.4 us -> none  [visit(): lax.dot_general(unit, visitor, (((1,), (1,)), ((), ())), preferred_elemen...]
    pallas_call x0 -> x3, Pallas kernels: none -> 5.43 us  [the longest x1 2.14 us: local(): pl.pallas_call(functools.partial(near_kernel, blocks), out_shape=(units,...]
  transfers between devices with their start and end apart: 15 -> 11, of which waited for: 15 -> 4; matrix products, arithmetic and copies ran while one was open for 1% -> 2% of each run, Pallas kernels for 0% -> 8%
where the time goes in v1:
time: 43.5 us; the launch traced here: 43.4 us
  waiting for transfers between devices  19.2 us (44%)
  starting transfers between devices  16.2 us (37%)
  Pallas kernels  5.43 us (12%)
  other arithmetic  1.26 us (3%)
  local copies, waits for them, and re-layouts  1.16 us (3%)
    ppermute x8, waiting for transfers between devices, swapped(): return lax.ppermute(array, 'shift', [(i, i ^ mask) for i in range(length)])  15.2 us
    ppermute x3, starting transfers between devices, moved(): return lax.ppermute(array, 'shift', pairs)  8.51 us
    ppermute x8, starting transfers between devices, swapped(): return lax.ppermute(array, 'shift', [(i, i ^ mask) for i in range(length)])  7.73 us
    ppermute x3, waiting for transfers between devices, moved(): return lax.ppermute(array, 'shift', pairs)  4.07 us
    pallas_call x1, Pallas kernels, local(): pl.pallas_call(functools.partial(near_kernel, blocks), out_shape=(units,...  2.14 us
    pallas_call x1, Pallas kernels, local(): pl.pallas_call(functools.partial(far_kernel, blocks), out_shape=(line, ja...  1.81 us
    pallas_call x1, Pallas kernels, local(): pl.pallas_call(functools.partial(partner_kernel, blocks), out_shape=(unit...  1.47 us
    unnamed x2, local copies, waits for them, and re-layouts  1.13 us
  transfers between devices with their start and end apart: 11, of which 4 were waited for; matrix products, arithmetic and copies ran while one was open for 2% of the time, Pallas kernels for 8%

profile of v1, /device:TPU:0, one launch (start us, length us, event | category | flops | bytes accessed | tf_op | source)
XLA Modules:
  0.0 43.4 jit_solution(1218572480220283515)
XLA Ops:
  0.0 3.0 %collective-permute-start.5 = (bf16[512,768]{1,0:T(8,128)(2,1)}, bf16[512,768]{1,0:T(8,128)(2,1)S(1)}, u32[]{:S(2)}, u32[]{:S(2)}) collective-permute-start(bf16[512,768]{1,0:T(8,128)(2,1)} %own_ref.1), channel_id=1, source_target_pairs={{0,2},{1,3},{2,0},{3,1},{4,6},{5,7},{6,4},{7,5},{8,10},{9,11},{10,... | collective-permute-start | bytes 2359304 | tf_op jit(solution)/shard_map/ppermute | solution.py:17
  3.0 0.0 collective-permute-start.4
  3.0 3.5 %collective-permute-start.7 = (bf16[512,768]{1,0:T(8,128)(2,1)}, bf16[512,768]{1,0:T(8,128)(2,1)S(1)}, u32[]{:S(2)}, u32[]{:S(2)}) collective-permute-start(bf16[512,768]{1,0:T(8,128)(2,1)} %own_ref.1), channel_id=1, source_target_pairs={{0,4},{1,5},{2,6},{3,7},{4,8},{5,9},{6,10},{7,11},{8,12},{9,13},{1... | collective-permute-start | bytes 2359304 | tf_op jit(solution)/shard_map/ppermute | solution.py:23
  6.5 14.2 %collective-permute-done.5.partner_ref = bf16[512,768]{1,0:T(8,128)(2,1)S(1)} collective-permute-done((bf16[512,768]{1,0:T(8,128)(2,1)}, bf16[512,768]{1,0:T(8,128)(2,1)S(1)}, u32[]{:S(2)}, u32[]{:S(2)}) %collective-permute-start.5) | collective-permute-done | bytes 786464 | tf_op jit(solution)/shard_map/ppermute | solution.py:17
  20.7 0.0 collective-permute-start.6
  20.7 0.7 %broadcast_add_fusion = (s32[4]{0:T(128)S(1)}, s32[1,4]{1,0:T(1,128)S(1)}) fusion(s32[4]{0:T(128)} %param.3), kind=kLoop, calls=%fused_computation.7 | loop fusion | flops 4 | bytes 48 | tf_op jit(solution)/shard_map/add | solution.py:141
  21.4 0.5 %collective-permute-start = (s32[4]{0:T(128)S(1)}, s32[4]{0:T(128)S(1)}, u32[]{:S(2)}, u32[]{:S(2)}) collective-permute-start(s32[4]{0:T(128)S(1)} %get-tuple-element.23), channel_id=1, source_target_pairs={{0,1},{1,0},{2,3},{3,2},{4,5},{5,4},{6,7},{7,6},{8,9},{9,8},{10,11... | collective-permute-start | bytes 56 | tf_op jit(solution)/shard_map/ppermute | solution.py:17
  21.9 1.7 %collective-permute-start.1 = (s32[4]{0:T(128)S(1)}, s32[4]{0:T(128)S(1)}, u32[]{:S(2)}, u32[]{:S(2)}) collective-permute-start(s32[4]{0:T(128)S(1)} %get-tuple-element.23), channel_id=1, source_target_pairs={{0,2},{1,3},{2,0},{3,1},{4,6},{5,7},{6,4},{7,5},{8,10},{9,11},{10,... | collective-permute-start | bytes 56 | tf_op jit(solution)/shard_map/ppermute | solution.py:17
  23.6 0.0 collective-permute-done
  23.6 0.9 %collective-permute-start.2 = (s32[4]{0:T(128)S(1)}, s32[4]{0:T(128)S(1)}, u32[]{:S(2)}, u32[]{:S(2)}) collective-permute-start(s32[4]{0:T(128)S(1)} %get-tuple-element.23), channel_id=1, source_target_pairs={{0,3},{1,2},{2,1},{3,0},{4,7},{5,6},{6,5},{7,4},{8,11},{9,10},{10,... | collective-permute-start | bytes 56 | tf_op jit(solution)/shard_map/ppermute | solution.py:17
  24.5 0.9 %collective-permute-done.1 = s32[4]{0:T(128)S(1)} collective-permute-done((s32[4]{0:T(128)S(1)}, s32[4]{0:T(128)S(1)}, u32[]{:S(2)}, u32[]{:S(2)}) %collective-permute-start.1) | collective-permute-done | bytes 48 | tf_op jit(solution)/shard_map/ppermute | solution.py:17
  25.4 3.7 %collective-permute-start.3 = (s32[4]{0:T(128)S(1)}, s32[4]{0:T(128)S(1)}, u32[]{:S(2)}, u32[]{:S(2)}) collective-permute-start(s32[4]{0:T(128)S(1)} %get-tuple-element.23), channel_id=1, source_target_pairs={{0,4},{1,5},{2,6},{3,7},{4,8},{5,9},{6,10},{7,11},{8,12},{9,13},{1... | collective-permute-start | bytes 56 | tf_op jit(solution)/shard_map/ppermute | solution.py:23
  29.1 0.0 collective-permute-done.2
  29.1 1.3 %collective-permute-done.3 = s32[4]{0:T(128)S(1)} collective-permute-done((s32[4]{0:T(128)S(1)}, s32[4]{0:T(128)S(1)}, u32[]{:S(2)}, u32[]{:S(2)}) %collective-permute-start.3) | collective-permute-done | bytes 48 | tf_op jit(solution)/shard_map/ppermute | solution.py:23
  30.4 0.0 copy-start
  30.4 1.1 %copy-done = bf16[512,768]{1,0:T(8,128)(2,1)S(1)} copy-done((bf16[512,768]{1,0:T(8,128)(2,1)S(1)}, bf16[512,768]{1,0:T(8,128)(2,1)}, u32[]{:S(2)}) %copy-start) | copy-done | bytes 786456
  31.6 2.1 %shard_map.28 = (bf16[512,768]{1,0:T(8,128)(2,1)S(1)}, bf16[512,768]{1,0:T(8,128)(2,1)S(1)}, f32[1,512]{1,0:T(1,128)S(1)}) custom-call(s32[5,4]{1,0:T(8,128)S(1)} %stack.23.ids, bf16[512,768]{1,0:T(8,128)(2,1)S(1)} %copy-done, bf16[512,768]{1,0:T(8,128)(2,1)S(1)} %collective-permute-done.4.mate_ref), custom_call_target="tpu_custom_call" | custom-call | flops 805306368 | bytes 3145728 | tf_op jit(solution)/shard_map/pallas_call | solution.py:159
  33.7 1.5 %shard_map.29 = (bf16[512,768]{1,0:T(8,128)(2,1)S(1)}, f32[1,512]{1,0:T(1,128)S(1)}) custom-call(s32[5,4]{1,0:T(8,128)S(1)} %stack.23.ids, bf16[512,768]{1,0:T(8,128)(2,1)S(1)} %get-tuple-element.13.own_unit, bf16[512,768]{1,0:T(8,128)(2,1)S(1)} %collective-permute-done.5.partner_ref, f32[1,512]{1,0:T(1,128)S(1)} %get-tuple-element.15.best_in), custom_call_target="tpu_custom_call" | custom-call | flops 402653184 | bytes 2359296 | tf_op jit(solution)/shard_map/pallas_call | solution.py:169
  35.2 1.8 %shard_map.30 = (f32[1,512]{1,0:T(1,128)S(1)}, f32[3,512]{1,0:T(4,128)S(1)}, f32[1,512]{1,0:T(1,128)S(1)}) custom-call(s32[5,4]{1,0:T(8,128)S(1)} %stack.23.ids, bf16[512,768]{1,0:T(8,128)(2,1)S(1)} %get-tuple-element.13.own_unit, bf16[512,768]{1,0:T(8,128)(2,1)S(1)} %get-tuple-element.14.mate_unit, bf16[512,768]{1,0:T(8,128)(2,1)S(1)} %get-tuple-element.16.partner_unit, ...), custom_call_target="tpu_custom_call" | custom-call | flops 2013265920 | bytes 3932160 | tf_op jit(solution)/shard_map/pallas_call | solution.py:178
  37.1 0.1 collective-permute-start.9
  37.1 1.3 %collective-permute-start.8 = (f32[1,512]{1,0:T(1,128)S(1)}, f32[1,512]{1,0:T(1,128)S(1)}, u32[]{:S(2)}, u32[]{:S(2)}) collective-permute-start(f32[1,512]{1,0:T(1,128)S(1)} %get-tuple-element.19), channel_id=1, source_target_pairs={{4,0},{5,1},{6,2},{7,3},{8,4},{9,5},{10,6},{11,7},{12,8},{13,9},{1... | collective-permute-start | bytes 6152 | tf_op jit(solution)/shard_map/ppermute | solution.py:23
  38.5 1.6 %collective-permute-start.10 = (f32[1,512]{1,0:T(1,128)S(1)}, f32[1,512]{1,0:T(1,128)S(1)}, u32[]{:S(2)}, u32[]{:S(2)}) collective-permute-start(f32[1,512]{1,0:T(1,128)S(1)} %slice_maximum_fusion), channel_id=1, source_target_pairs={{0,2},{1,3},{2,0},{3,1},{4,6},{5,7},{6,4},{7,5},{8,10},{9,11},{10,... | collective-permute-start | bytes 6152 | tf_op jit(solution)/shard_map/ppermute | solution.py:17
  40.1 2.8 %collective-permute-done.8 = f32[1,512]{1,0:T(1,128)S(1)} collective-permute-done((f32[1,512]{1,0:T(1,128)S(1)}, f32[1,512]{1,0:T(1,128)S(1)}, u32[]{:S(2)}, u32[]{:S(2)}) %collective-permute-start.8) | collective-permute-done | bytes 2080 | tf_op jit(solution)/shard_map/ppermute | solution.py:23
  42.9 0.6 %fusion.2 = f32[1,512]{1,0:T(1,128)} fusion(f32[1,512]{1,0:T(1,128)S(1)} %collective-permute-done.10, f32[2,512]{1,0:T(2,128)S(1)} %collective-permute-done.9, f32[1,512]{1,0:T(1,128)S(1)} %get-tuple-element.18, f32[1,512]{1,0:T(1,128)S(1)} %collective-permute-done.8, pred[]{:T(512)S(6)} %lt.3), kind=kLoop, calls=%fused_computation.6 | loop fusion | flops 2560 | bytes 10241 | tf_op jit(solution)/shard_map/max | solution.py:196
  (9 shorter events, 0.1 us)
Async XLA Ops:
  0.0 20.7 %collective-permute-start.5 = (bf16[512,768]{1,0:T(8,128)(2,1)}, bf16[512,768]{1,0:T(8,128)(2,1)S(1)}, u32[]{:S(2)}, u32[]{:S(2)}) collective-permute-start(bf16[512,768]{1,0:T(8,128)(2,1)} %own_ref.1), channel_id=1, source_target_pairs={{0,2},{1,3},{2,0},{3,1},{4,6},{5,7},{6,4},{7,5},{8,10},{9,11},{10,... | collective-permute-start | bytes 2359304 | tf_op jit(solution)/shard_map/ppermute | solution.py:17
  3.0 27.5 %collective-permute-start.4 = (bf16[512,768]{1,0:T(8,128)(2,1)}, bf16[512,768]{1,0:T(8,128)(2,1)S(1)}, u32[]{:S(2)}, u32[]{:S(2)}) collective-permute-start(bf16[512,768]{1,0:T(8,128)(2,1)} %own_ref.1), channel_id=1, source_target_pairs={{0,1},{1,0},{2,3},{3,2},{4,5},{5,4},{6,7},{7,6},{8,9},{9,8},{10,11... | collective-permute-start | bytes 2359304 | tf_op jit(solution)/shard_map/ppermute | solution.py:17
  3.0 32.2 %collective-permute-start.7 = (bf16[512,768]{1,0:T(8,128)(2,1)}, bf16[512,768]{1,0:T(8,128)(2,1)S(1)}, u32[]{:S(2)}, u32[]{:S(2)}) collective-permute-start(bf16[512,768]{1,0:T(8,128)(2,1)} %own_ref.1), channel_id=1, source_target_pairs={{0,4},{1,5},{2,6},{3,7},{4,8},{5,9},{6,10},{7,11},{8,12},{9,13},{1... | collective-permute-start | bytes 2359304 | tf_op jit(solution)/shard_map/ppermute | solution.py:23
  20.7 14.5 %collective-permute-start.6 = (bf16[512,768]{1,0:T(8,128)(2,1)S(1)}, bf16[512,768]{1,0:T(8,128)(2,1)S(1)}, u32[]{:S(2)}, u32[]{:S(2)}) collective-permute-start(bf16[512,768]{1,0:T(8,128)(2,1)S(1)} %collective-permute-done.5.partner_ref), channel_id=1, source_target_pairs={{0,1},{1,0},{2,3},{3,2},{4,5},{5,4},{6,7},{7,6},{8,9},{9,8},{10,11... | collective-permute-start | bytes 2359304 | tf_op jit(solution)/shard_map/ppermute | solution.py:17
  21.4 2.3 %collective-permute-start = (s32[4]{0:T(128)S(1)}, s32[4]{0:T(128)S(1)}, u32[]{:S(2)}, u32[]{:S(2)}) collective-permute-start(s32[4]{0:T(128)S(1)} %get-tuple-element.23), channel_id=1, source_target_pairs={{0,1},{1,0},{2,3},{3,2},{4,5},{5,4},{6,7},{7,6},{8,9},{9,8},{10,11... | collective-permute-start | bytes 56 | tf_op jit(solution)/shard_map/ppermute | solution.py:17
  21.9 3.5 %collective-permute-start.1 = (s32[4]{0:T(128)S(1)}, s32[4]{0:T(128)S(1)}, u32[]{:S(2)}, u32[]{:S(2)}) collective-permute-start(s32[4]{0:T(128)S(1)} %get-tuple-element.23), channel_id=1, source_target_pairs={{0,2},{1,3},{2,0},{3,1},{4,6},{5,7},{6,4},{7,5},{8,10},{9,11},{10,... | collective-permute-start | bytes 56 | tf_op jit(solution)/shard_map/ppermute | solution.py:17
  23.6 5.5 %collective-permute-start.2 = (s32[4]{0:T(128)S(1)}, s32[4]{0:T(128)S(1)}, u32[]{:S(2)}, u32[]{:S(2)}) collective-permute-start(s32[4]{0:T(128)S(1)} %get-tuple-element.23), channel_id=1, source_target_pairs={{0,3},{1,2},{2,1},{3,0},{4,7},{5,6},{6,5},{7,4},{8,11},{9,10},{10,... | collective-permute-start | bytes 56 | tf_op jit(solution)/shard_map/ppermute | solution.py:17
  25.4 5.0 %collective-permute-start.3 = (s32[4]{0:T(128)S(1)}, s32[4]{0:T(128)S(1)}, u32[]{:S(2)}, u32[]{:S(2)}) collective-permute-start(s32[4]{0:T(128)S(1)} %get-tuple-element.23), channel_id=1, source_target_pairs={{0,4},{1,5},{2,6},{3,7},{4,8},{5,9},{6,10},{7,11},{8,12},{9,13},{1... | collective-permute-start | bytes 56 | tf_op jit(solution)/shard_map/ppermute | solution.py:23
  30.4 1.1 %copy-start = (bf16[512,768]{1,0:T(8,128)(2,1)S(1)}, bf16[512,768]{1,0:T(8,128)(2,1)}, u32[]{:S(2)}) copy-start(bf16[512,768]{1,0:T(8,128)(2,1)} %own_ref.1) | copy-start | bytes 2359300
  37.1 1.4 %collective-permute-start.9 = (f32[2,512]{1,0:T(2,128)S(1)}, f32[2,512]{1,0:T(2,128)S(1)}, u32[]{:S(2)}, u32[]{:S(2)}) collective-permute-start(f32[2,512]{1,0:T(2,128)S(1)} %pad_maximum_fusion), channel_id=1, source_target_pairs={{0,1},{1,0},{2,3},{3,2},{4,5},{5,4},{6,7},{7,6},{8,9},{9,8},{10,11... | collective-permute-start | bytes 12296 | tf_op jit(solution)/shard_map/ppermute | solution.py:17
  37.1 5.7 %collective-permute-start.8 = (f32[1,512]{1,0:T(1,128)S(1)}, f32[1,512]{1,0:T(1,128)S(1)}, u32[]{:S(2)}, u32[]{:S(2)}) collective-permute-start(f32[1,512]{1,0:T(1,128)S(1)} %get-tuple-element.19), channel_id=1, source_target_pairs={{4,0},{5,1},{6,2},{7,3},{8,4},{9,5},{10,6},{11,7},{12,8},{13,9},{1... | collective-permute-start | bytes 6152 | tf_op jit(solution)/shard_map/ppermute | solution.py:23
  38.5 4.4 %collective-permute-start.10 = (f32[1,512]{1,0:T(1,128)S(1)}, f32[1,512]{1,0:T(1,128)S(1)}, u32[]{:S(2)}, u32[]{:S(2)}) collective-permute-start(f32[1,512]{1,0:T(1,128)S(1)} %slice_maximum_fusion), channel_id=1, source_target_pairs={{0,2},{1,3},{2,0},{3,1},{4,6},{5,7},{6,4},{7,5},{8,10},{9,11},{10,... | collective-permute-start | bytes 6152 | tf_op jit(solution)/shard_map/ppermute | solution.py:17
